TPU v7x, 32 devices: a whole 2x2x4 slice. The times are simulated.
32 devices in a mesh: leaf: 8 (over y, x, core), row: 4 (over z).
Axes of the slice: x: 2, y: 2, z: 4, core: 2. Of those that a mesh axis runs over, the one named last changes fastest.
Arguments:
- leaf_cost: float32 [8, 2048, 2048], P('leaf', 'row'), as said below
- a_blocks: float32 [8, 16, 8, 128, 128], P('leaf'), may hold values from -0.046875 to 0.046875
- a_cols: int32 [8, 16, 8], P('leaf'), may hold values from 0 to 15, as said below
- b_blocks: float32 [8, 16, 2, 128, 128], P('leaf'), may hold values from -0.1875 to 0.1875
- b_cols: int32 [8, 16, 2], P('leaf'), may hold values from 0 to 3, as said below
- branch_prob: float32 [8], P('leaf'), may hold values from 0.3 to 0.7
- state_cost: float32 [2048], P('row'), may hold values from 0.5 to 2
- control_cost: float32 [512], replicated, may hold values from 0.5 to 2
- parent_state: float32 [4, 2048, 128], P(None, 'row'), may hold values from -6 to 6
Outputs:
- parent_cost: float32 [8, 2048, 2048], P('leaf', 'row')
- gains: float32 [8, 512, 2048], P('leaf', None, 'row')
- child_state: float32 [8, 2048, 128], P('leaf', 'row')
Inputs may be any that keep to these rules, and one draw needn't show every extreme that they name: a_cols[c, k, 0] equals k, and the 8 entries of one block row are distinct. `b_cols`: the 2 entries of one block row are distinct. Each leaf_cost[c] is symmetric with a diagonal of 2 to 4.
All inputs are finite; a program needn't handle non-finite values.
Results may differ from a plain program's by a relative error of at most 0.0003.
Values sent between devices are 32-bit elements; how exact they have to be, the bound alone decides.
No kernel may reach another device: no remote copies, remote signals or barrier semaphores. Data moves between devices by JAX's collectives and lax.ppermute only.
A program may use at most 256 MiB of HBM per device.

v0:
```python
import jax
import jax.numpy as jnp
from jax import lax
from jax.sharding import PartitionSpec as P

HIGH = lax.Precision.HIGHEST


def swapped(x, axis, bit):
    return lax.ppermute(x, axis, [(i, i ^ 1 << bit) for i in range(lax.axis_size(axis))])


def lower_solve(factor, rhs):
    return lax.linalg.triangular_solve(factor, rhs, left_side=True, lower=True)


def upper_solve(factor, rhs):
    return lax.linalg.triangular_solve(factor, rhs, left_side=True, lower=True, transpose_a=True)


def shards(
    leaf_cost,
    a_blocks,
    a_cols,
    b_blocks,
    b_cols,
    branch_prob,
    state_cost,
    control_cost,
    parent_state,
):
    rows = leaf_cost.shape[1]
    width = leaf_cost.shape[2]
    blk = a_blocks.shape[3]
    nbx = width // blk
    local_blocks = rows // blk
    orders = control_cost.shape[0]
    nbu = orders // blk
    row_index = lax.axis_index("row")
    leaf_index = lax.axis_index("leaf")
    own_state = lax.dynamic_index_in_dim(parent_state, leaf_index // 2, 0, keepdims=False)
    full_state = lax.all_gather(own_state, "row", axis=0, tiled=True)
    cost_rows = leaf_cost[0]
    weight = branch_prob[0]
    ident = jnp.eye(blk, dtype=jnp.float32)
    a_all = a_blocks[0].at[:, 0].add(0.75 * ident)
    b_all = b_blocks[0]
    a_index = a_cols[0]
    b_index = b_cols[0]
    a_onehot = (a_index[..., None] == jnp.arange(nbx)[None, None, :]).astype(jnp.float32)
    b_onehot = (b_index[..., None] == jnp.arange(nbu)[None, None, :]).astype(jnp.float32)
    cost_split = cost_rows.reshape(rows, nbx, blk)
    a_pieces = jnp.einsum("rkb,ksbc->ksrc", cost_split, a_all, precision=HIGH)
    image = jnp.einsum("ksj,ksrc->rjc", a_onehot, a_pieces, precision=HIGH).reshape(rows, width)
    b_pieces = jnp.einsum("rkb,ksbc->ksrc", cost_split, b_all, precision=HIGH)
    wimage = jnp.einsum("ksj,ksrc->rjc", b_onehot, b_pieces, precision=HIGH).reshape(rows, orders)
    first = row_index * local_blocks
    a_mine = lax.dynamic_slice_in_dim(a_all, first, local_blocks, 0)
    b_mine = lax.dynamic_slice_in_dim(b_all, first, local_blocks, 0)
    a_hot_mine = lax.dynamic_slice_in_dim(a_onehot, first, local_blocks, 0)
    b_hot_mine = lax.dynamic_slice_in_dim(b_onehot, first, local_blocks, 0)
    a_idx_mine = lax.dynamic_slice_in_dim(a_index, first, local_blocks, 0)
    b_idx_mine = lax.dynamic_slice_in_dim(b_index, first, local_blocks, 0)
    image_blocks = image.reshape(local_blocks, blk, width)
    a_terms = jnp.einsum("ksbc,kbn->kscn", a_mine, image_blocks, precision=HIGH)
    state_part = weight * jnp.einsum("ksj,kscn->jcn", a_hot_mine, a_terms, precision=HIGH).reshape(
        width, width
    )
    b_terms = jnp.einsum("ksbc,kbn->kscn", b_mine, image_blocks, precision=HIGH)
    cross_part = weight * jnp.einsum("ksj,kscn->jcn", b_hot_mine, b_terms, precision=HIGH).reshape(
        orders, width
    )
    g_terms = jnp.einsum(
        "ksbc,kbn->kscn", b_mine, wimage.reshape(local_blocks, blk, orders), precision=HIGH
    )
    gram_part = weight * jnp.einsum("ksj,kscn->jcn", b_hot_mine, g_terms, precision=HIGH).reshape(
        orders, orders
    )
    state_sum = lax.psum_scatter(state_part, "row", scatter_dimension=0, tiled=True)
    cross_sum, gram_sum = lax.psum((cross_part, gram_part), "row")
    other_state, other_cross, other_gram = swapped((state_sum, cross_sum, gram_sum), "leaf", 0)
    state_sum = state_sum + other_state
    cross_sum = cross_sum + other_cross
    gram_sum = gram_sum + other_gram
    global_rows = row_index * rows + jnp.arange(rows)
    diag_rows = (jnp.arange(width)[None, :] == global_rows[:, None]).astype(
        jnp.float32
    ) * state_cost[:, None]
    state_total = state_sum + diag_rows
    gram_total = gram_sum + jnp.diag(control_cost)
    factor = jnp.linalg.cholesky(gram_total)
    solved = lower_solve(factor, cross_sum)
    solved_mine = lax.dynamic_slice_in_dim(solved, row_index * rows, rows, 1)
    pcost_rows = state_total - jnp.dot(solved_mine.T, solved, precision=HIGH)
    gain_cols = -upper_solve(factor, solved_mine)
    control = lax.psum(jnp.dot(gain_cols, own_state, precision=HIGH), "row")
    state_blocks = full_state.reshape(nbx, blk, -1)
    picked_state = jnp.take(state_blocks, a_idx_mine, axis=0)
    control_blocks = control.reshape(nbu, blk, -1)
    picked_control = jnp.take(control_blocks, b_idx_mine, axis=0)
    reached = jnp.einsum("ksbc,kscm->kbm", a_mine, picked_state, precision=HIGH)
    reached = reached + jnp.einsum("ksbc,kscm->kbm", b_mine, picked_control, precision=HIGH)
    next_rows = reached.reshape(rows, -1)
    return (pcost_rows[None], gain_cols[None], next_rows[None])


def solution(mesh):
    placed = (
        P("leaf", "row", None),
        P("leaf", None, None, None, None),
        P("leaf", None, None),
        P("leaf", None, None, None, None),
        P("leaf", None, None),
        P("leaf"),
        P("row"),
        P(),
        P(None, "row", None),
    )
    return jax.shard_map(
        shards,
        mesh=mesh,
        in_specs=placed,
        out_specs=(P("leaf", "row", None), P("leaf", None, "row"), P("leaf", "row", None)),
        check_vma=False,
    )
```

profile of v0, /device:TPU:0, one launch (start us, length us, event | category | flops | bytes accessed | tf_op | source)
XLA Modules:
  0.0 752.5 jit_solution(1161826850676851788)
XLA Ops:
  15.0 10.7 %fusion.23 = f32[16,2,128,512]{3,2,1,0:T(8,128)} fusion(f32[512,16,128,1]{0,2,3,1:T(8,128)} %bitcast.179, f32[1,16,2,128,128]{4,3,2,1,0:T(8,128)S(1)} %copy-done), kind=kOutput, calls=%fused_computation.28 | convolution fusion | flops 3221225472 | bytes 14680064 | tf_op jit(solution)/shard_map/rkb,ksbc->ksrc/dot_general | solution.py:55
  25.7 10.4 %copy.53 = f32[16,2,128,512]{2,0,1,3:T(8,128)} copy(f32[16,2,128,512]{3,2,1,0:T(8,128)} %fusion.23) | data formatting | bytes 16777216 | tf_op jit(solution)/shard_map/rkb,ksbc->ksrc/dot_general | solution.py:55
  61.3 31.5 %fusion.125 = f32[16,8,128,512]{3,2,1,0:T(8,128)} fusion(f32[16,8,128,128]{3,2,1,0:T(8,128)S(1)} %fusion.54, f32[512,16,128,1]{0,2,3,1:T(8,128)S(1)} %bitcast.180), kind=kOutput, calls=%fused_computation.179 | convolution fusion | flops 12884901888 | bytes 46137344 | tf_op jit(solution)/shard_map/rkb,ksbc->ksrc/dot_general | solution.py:53
  92.8 34.5 %copy.49 = f32[16,8,128,512]{2,0,1,3:T(8,128)} copy(f32[16,8,128,512]{3,2,1,0:T(8,128)} %fusion.125) | data formatting | bytes 67108864 | tf_op jit(solution)/shard_map/rkb,ksbc->ksrc/dot_general | solution.py:53
  127.3 18.8 %fusion.16 = f32[512,16,128]{2,1,0:T(8,128)} fusion(f32[16,8,128,512]{2,0,1,3:T(8,128)} %copy.49, pred[16,8,16]{0,2,1:T(8,128)(4,1)S(1)} %copy.31), kind=kOutput, calls=%fused_computation.23 | convolution fusion | flops 1610612736 | bytes 37750784 | tf_op jit(solution)/shard_map/ksj,ksrc->rjc/dot_general | solution.py:54
  151.0 9.3 %fusion.6 = f32[4,2,128,2048]{3,2,1,0:T(8,128)S(1)} fusion(f32[4,128,2048,1]{2,1,0,3:T(8,128)} %reshape.288, f32[1,16,2,128,128]{4,3,2,1,0:T(8,128)S(1)} %copy-done, s32[]{:T(128)S(6)} %select_n.69), kind=kOutput, calls=%fused_computation.13 | convolution fusion | flops 3221225472 | bytes 13107204 | tf_op jit(solution)/shard_map/ksbc,kbn->kscn/dot_general | solution.py:69
  160.3 11.4 %bitcast_multiply_fusion.1 = f32[4,128,2048]{2,0,1:T(4,128)S(1)} fusion(f32[4,2,128,2048]{3,2,1,0:T(8,128)S(1)} %fusion.6, f32[]{:T(128)} %bitcast.177, pred[16,2,4]{0,2,1:T(4,128)(4,1)S(1)} %iota_compare_fusion.6, s32[]{:T(128)S(6)} %select_n.69), kind=kOutput, calls=%fused_computation.12 | convolution fusion | flops 101711872 | bytes 12583048 | tf_op jit(solution)/shard_map/ksj,kscn->jcn/dot_general | solution.py:70
  184.4 31.8 %fusion.126 = f32[4,8,128,2048]{3,1,0,2:T(8,128)} fusion(f32[4,8,128,128]{2,1,0,3:T(8,128)} %copy.51, f32[4,128,2048,1]{2,1,0,3:T(8,128)} %reshape.288), kind=kOutput, calls=%fused_computation.180 | convolution fusion | flops 12884901888 | bytes 39845888 | tf_op jit(solution)/shard_map/ksbc,kbn->kscn/dot_general | solution.py:65
  216.2 17.2 %bitcast_multiply_fusion = f32[16,128,2048]{2,0,1:T(8,128)S(1)} fusion(f32[]{:T(128)} %bitcast.175, f32[4,8,128,2048]{3,1,0,2:T(8,128)} %fusion.126, pred[16,8,16]{2,1,0:T(8,128)(4,1)S(1)} %iota_compare_fusion.5, s32[]{:T(128)S(6)} %select_n.69), kind=kOutput, calls=%fused_computation.6 | convolution fusion | flops 1614807040 | bytes 50335752 | tf_op jit(solution)/shard_map/ksj,kscn->jcn/dot_general | solution.py:66
  233.4 18.4 %copy.32 = f32[16,128,2048]{2,1,0:T(8,128)} copy(f32[16,128,2048]{2,0,1:T(8,128)S(1)} %bitcast_multiply_fusion) | data formatting | bytes 33554432 | tf_op jit(solution)/shard_map/mul | solution.py:66
  252.4 115.9 %all-reduce.7.cloned.1.call-done = (f32[512,2048]{1,0:T(8,128)}, f32[512,512]{0,1:T(8,128)}) async-done(((f32[512,2048]{1,0:T(8,128)}, f32[512,512]{0,1:T(8,128)}), (f32[512,2048]{1,0:T(8,128)}, f32[512,512]{0,1:T(8,128)})) %all-reduce.7.cloned.1.call-update) | async-done | bytes 5242896 | tf_op jit(solution)/shard_map/psum | solution.py:80
  370.1 26.8 %all-gather.3.cloned.1.call-done = f32[1,2048,128]{2,1,0:T(8,128)} async-done(((f32[1,512,128]{2,1,0:T(8,128)}), f32[1,2048,128]{2,1,0:T(8,128)}) %all-gather.3.cloned.1.call-update) | async-done | bytes 1048592 | tf_op jit(solution)/shard_map/all_gather | solution.py:42
  405.5 11.7 %cholesky.84 = f32[128,128]{1,0:T(8,128)S(1)} custom-call(f32[128,128]{1,0:T(8,128)S(1)} %cholesky.226), custom_call_target="Cholesky" | custom-call | tf_op jit(solution)/shard_map/jit(cholesky)/cholesky | solution.py:91
  417.3 9.8 %custom-call.32 = f32[1,128,128]{1,2,0:T(8,128)S(1)} custom-call(f32[1,128,128]{2,1,0:T(8,128)S(1)} %get-tuple-element.48), custom_call_target="InvertDiagBlocksLowerTriangular" | custom-call | tf_op jit(solution)/shard_map/jit(cholesky)/cholesky | solution.py:91
  430.5 11.7 %cholesky.178 = f32[128,128]{1,0:T(8,128)S(1)} custom-call(f32[128,128]{1,0:T(8,128)S(1)} %cholesky.230), custom_call_target="Cholesky" | custom-call | tf_op jit(solution)/shard_map/jit(cholesky)/cholesky | solution.py:91
  443.5 10.6 %custom-call.33 = f32[1,128,128]{1,2,0:T(8,128)} custom-call(f32[1,128,128]{2,1,0:T(8,128)S(1)} %get-tuple-element.46), custom_call_target="InvertDiagBlocksLowerTriangular" | custom-call | tf_op jit(solution)/shard_map/jit(cholesky)/cholesky | solution.py:91
  458.6 11.7 %cholesky.199 = f32[128,128]{1,0:T(8,128)S(1)} custom-call(f32[128,128]{1,0:T(8,128)S(1)} %cholesky.235), custom_call_target="Cholesky" | custom-call | tf_op jit(solution)/shard_map/jit(cholesky)/cholesky | solution.py:91
  470.4 9.8 %custom-call.34 = f32[1,128,128]{1,2,0:T(8,128)S(1)} custom-call(f32[1,128,128]{2,1,0:T(8,128)S(1)} %get-tuple-element.44), custom_call_target="InvertDiagBlocksLowerTriangular" | custom-call | tf_op jit(solution)/shard_map/jit(cholesky)/cholesky | solution.py:91
  481.9 11.9 %cholesky.216 = f32[128,128]{1,0:T(8,128)S(1)} custom-call(f32[128,128]{1,0:T(8,128)S(1)} %convolution_subtract_fusion.5), custom_call_target="Cholesky" | custom-call | tf_op jit(solution)/shard_map/jit(cholesky)/cholesky | solution.py:91
  500.8 14.6 %while.2 = (s32[]{:T(128)}, f32[512,512]{0,1:T(8,128)}, s32[4,2]{0,1:T(2,128)S(1)}, f32[4,128,128]{2,1,0:T(8,128)}, s32[]{:T(128)}) while((s32[]{:T(128)}, f32[512,512]{0,1:T(8,128)}, s32[4,2]{0,1:T(2,128)S(1)}, f32[4,128,128]{2,1,0:T(8,128)}, s32[]{:T(128)}) %tuple.33), condition=%wide.while_cond.1, body=%wide.while_body.1.sunk | while | flops 2 | bytes 393329 | solution.py:14
  515.4 40.1 %custom-call.35 = f32[4,128,128]{1,2,0:T(8,128)S(1)} custom-call(f32[4,128,128]{2,1,0:T(8,128)} %get-tuple-element.22), custom_call_target="InvertDiagBlocksLowerTriangular" | custom-call | tf_op jit(solution)/shard_map/triangular_solve | solution.py:14
  565.7 113.3 %reduce-scatter.2.cloned.1.call-done = f32[512,2048]{1,0:T(8,128)} async-done(((f32[2048,2048]{1,0:T(8,128)}), f32[512,2048]{1,0:T(8,128)}) %reduce-scatter.2.cloned.1.call-update) | async-done | bytes 4194320 | tf_op jit(solution)/shard_map/reduce_scatter | solution.py:79
  699.3 30.8 %all-reduce.5.cloned.1.call-done = f32[4,128,128]{2,1,0:T(8,128)} async-done(((f32[4,128,128]{2,1,0:T(8,128)}), f32[4,128,128]{2,1,0:T(8,128)}) %all-reduce.5.cloned.1.call-update) | async-done | bytes 262160 | tf_op jit(solution)/shard_map/psum | solution.py:96
  733.1 12.4 %subtract_bitcast_fusion = f32[1,512,2048]{2,1,0:T(8,128)} fusion(f32[512,2048]{1,0:T(8,128)} %reduce-scatter.2.cloned.1.call-done, f32[512,2048]{1,0:T(8,128)} %collective-permute-done, f32[512]{0:T(512)S(1)} %copy-done.13, s32[512]{0:T(512)S(1)} %iota_add_fusion, f32[512,2048]{1,0:T(8,128)} %copy-done.3, s32[]{:T(128)S(6)} %select_n.72), kind=kOutput, calls=%fused_computation.15 | convolution fusion | flops 6447693824 | bytes 17829892 | tf_op jit(solution)/shard_map/dot_general | solution.py:94
  (153 shorter events, 123.7 us)
Async XLA Ops:
  7.2 7.9 %copy-start = (f32[1,16,2,128,128]{4,3,2,1,0:T(8,128)S(1)}, f32[1,16,2,128,128]{4,3,2,1,0:T(8,128)}, u32[]{:S(2)}) copy-start(f32[1,16,2,128,128]{4,3,2,1,0:T(8,128)} %param.14) | copy-start | bytes 6291460
  7.2 361.1 %all-reduce.7.cloned.1.call-start = ((), (), s32[]{:S(2)}) async-start(), calls=%async_computation.4 | async-start | bytes 10485760 | tf_op jit(solution)/shard_map/psum | solution.py:80
  25.7 10.4 %copy-start.11 = (s32[1,16,2]{1,2,0:T(2,128)S(1)}, s32[1,16,2]{1,2,0:T(2,128)}, u32[]{:S(2)}) copy-start(s32[1,16,2]{1,2,0:T(2,128)} %param.15) | copy-start | bytes 388
  53.1 8.2 %copy-start.2 = (f32[1,512,2048]{1,2,0:T(8,128)S(1)}, f32[1,512,2048]{1,2,0:T(8,128)}, u32[]{:S(2)}) copy-start(f32[1,512,2048]{1,2,0:T(8,128)} %copy.65) | copy-start | bytes 12582916
  58.1 3.2 copy-start.1
  176.2 220.6 %all-gather.3.cloned.1.call-start = ((), (), s32[]{:S(2)}) async-start(), calls=%async_computation.3 | async-start | bytes 1310720 | tf_op jit(solution)/shard_map/all_gather | solution.py:42
  178.0 501.1 %reduce-scatter.2.cloned.1.call-start = ((), (), s32[]{:S(2)}) async-start(), calls=%async_computation.1 | async-start | bytes 20971520 | tf_op jit(solution)/shard_map/reduce_scatter | solution.py:79
  251.8 117.4 %copy-start.12 = (s32[1,16,8]{1,2,0:T(8,128)S(1)}, s32[1,16,8]{1,2,0:T(8,128)}, u32[]{:S(2)}) copy-start(s32[1,16,8]{1,2,0:T(8,128)} %param.13) | copy-start | bytes 1540
  251.8 148.2 %copy-start.14 = (f32[512]{0:T(512)S(1)}, f32[512]{0:T(512)}, u32[]{:S(2)}) copy-start(f32[512]{0:T(512)} %param.18) | copy-start | bytes 6148
  251.9 478.3 %all-reduce.5.cloned.1.call-start = ((), (), s32[]{:S(2)}) async-start(), calls=%async_computation.2 | async-start | bytes 524288 | tf_op jit(solution)/shard_map/psum | solution.py:96
  368.3 31.7 %collective-permute-start.1 = (f32[512,512]{0,1:T(8,128)}, f32[512,512]{0,1:T(8,128)}, u32[]{:S(2)}, u32[]{:S(2)}) collective-permute-start(f32[512,512]{0,1:T(8,128)} %get-tuple-element.40), channel_id=1, source_target_pairs={{0,4},{4,0},{8,12},{12,8},{16,20},{20,16},{24,28},{28,24},{1,5},{5... | collective-permute-start | bytes 3145736 | tf_op jit(solution)/shard_map/ppermute | solution.py:10
  400.0 155.5 %collective-permute-start.2 = (f32[512,2048]{1,0:T(8,128)}, f32[512,2048]{1,0:T(8,128)}, u32[]{:S(2)}, u32[]{:S(2)}) collective-permute-start(f32[512,2048]{1,0:T(8,128)} %get-tuple-element.39), channel_id=1, source_target_pairs={{0,4},{4,0},{8,12},{12,8},{16,20},{20,16},{24,28},{28,24},{1,5},{5... | collective-permute-start | bytes 12582920 | tf_op jit(solution)/shard_map/ppermute | solution.py:10
  404.5 1.0 copy-start.7
  559.8 2.0 copy-start.4
  679.1 4.9 copy-start.5
  679.1 6.0 copy-start.6
  679.1 54.0 %collective-permute-start = (f32[512,2048]{1,0:T(8,128)}, f32[512,2048]{1,0:T(8,128)}, u32[]{:S(2)}, u32[]{:S(2)}) collective-permute-start(f32[512,2048]{1,0:T(8,128)} %reduce-scatter.2.cloned.1.call-done), channel_id=1, source_target_pairs={{0,4},{4,0},{8,12},{12,8},{16,20},{20,16},{24,28},{28,24},{1,5},{5... | collective-permute-start | bytes 12582920 | tf_op jit(solution)/shard_map/ppermute | solution.py:10
  688.6 2.0 copy-start.3
  688.7 3.0 copy-start.8
  691.6 2.0 copy-start.9
  693.6 38.0 %copy-start.15 = (pred[4,2]{1,0:T(4,128)(4,1)S(1)}, pred[4,2]{1,0:T(4,128)(4,1)}, u32[]{:S(2)}) copy-start(pred[4,2]{1,0:T(4,128)(4,1)} %copy.46) | copy-start | bytes 28
  693.6 4.6 copy-start.10
  693.7 39.5 %copy-start.13 = (f32[512]{0:T(512)S(1)}, f32[512]{0:T(512)}, u32[]{:S(2)}) copy-start(f32[512]{0:T(512)} %param.17) | copy-start | bytes 6148
Sparse Core Ops, SparseCore 0:
  176.3 191.9 all-reduce.6
  369.9 26.8 all-gather.2
  399.2 279.8 reduce-scatter.1
  693.8 36.3 all-reduce.4
where the time goes:
time: 763 us; the launch traced here: 752 us
  waiting for transfers between devices  287 us (38%)
  matrix products  187 us (25%)
  other arithmetic  134 us (18%)
  local copies, waits for them, and re-layouts  127 us (17%)
  between operations  18.1 us (2%)
    psum x1, waiting for transfers between devices, shards(): cross_sum, gram_sum = lax.psum((cross_part, gram_part), 'row')  116 us
    reduce_scatter x1, waiting for transfers between devices, shards(): lax.psum_scatter(state_part, 'row', scatter_dimension=0, tiled=True)  113 us
    another operation x14, other arithmetic, shards(): factor = jnp.linalg.cholesky(gram_total)  80.4 us
    another operation x4, other arithmetic, lower_solve(): return lax.linalg.triangular_solve(factor, rhs, left_side=True, lower=True)  42.3 us
    dot_general x1, local copies, waits for them, and re-layouts, shards(): a_pieces = jnp.einsum('rkb,ksbc->ksrc', cost_split, a_all, precision=HIGH)  34.5 us
    dot_general x1, matrix products, shards(): a_terms = jnp.einsum('ksbc,kbn->kscn', a_mine, image_blocks, precision=HIGH)  31.8 us
    dot_general x1, matrix products, shards(): a_pieces = jnp.einsum('rkb,ksbc->ksrc', cost_split, a_all, precision=HIGH)  31.5 us
    psum x1, waiting for transfers between devices, shards(): control = lax.psum(jnp.dot(gain_cols, own_state, precision=HIGH), 'row')  30.8 us
  transfers between devices with their start and end apart: 7, of which 4 were waited for; matrix products, arithmetic and copies ran while one was open for 35% of the time, Pallas kernels for 0%

commit v1 on v0

v1 whole, which is shorter than its diff:
```python
import functools

import jax
import jax.numpy as jnp
from jax import lax
from jax.experimental import pallas as pl
from jax.experimental.pallas import tpu as pltpu
from jax.sharding import PartitionSpec as P

HIGHEST = lax.Precision.HIGHEST
F32 = jnp.float32
BF16 = jnp.bfloat16
VMEM_LIMIT = 48 * 2**20
NN = (((1,), (0,)), ((), ()))
NT = (((1,), (1,)), ((), ()))
TN = (((0,), (0,)), ((), ()))


def split(x):
    hi = x.astype(BF16)
    return hi, (x - hi.astype(F32)).astype(BF16)


def parted(x):
    hi = lax.reduce_precision(x, 8, 7)
    return hi.astype(BF16), (x - hi).astype(BF16)


def dot3(a, b, dims=NN):
    one = functools.partial(lax.dot_general, dimension_numbers=dims, preferred_element_type=F32)
    return one(a[0], b[0]) + (one(a[0], b[1]) + one(a[1], b[0]))


def dense_kernel(blk, step, nnza, nnzb, width, acol, bcol, a_ref, b_ref, p_ref, fh, fl, ph, pl_, w_ref, buf):
    i = pl.program_id(0)
    buf[...] = jnp.zeros_like(buf)
    diag = lax.broadcasted_iota(jnp.int32, (blk, blk), 0) == lax.broadcasted_iota(jnp.int32, (blk, blk), 1)
    eye = jnp.where(diag, 0.75, 0.0).astype(F32)
    for t in range(step // blk):
        row = i * (step // blk) + t
        for s in range(nnza):
            col = pl.multiple_of(acol[row * nnza + s] * blk, blk)
            block = a_ref[t, s]
            if s == 0:
                block = block + eye
            buf[t * blk : (t + 1) * blk, pl.ds(col, blk)] = block
        for s in range(nnzb):
            col = pl.multiple_of(width + bcol[row * nnzb + s] * blk, blk)
            buf[t * blk : (t + 1) * blk, pl.ds(col, blk)] = b_ref[t, s]
    hi, lo = split(buf[...])
    fh[...] = hi
    fl[...] = lo
    phi, plo = split(p_ref[...])
    ph[...] = phi
    pl_[...] = plo
    part = dot3((phi, plo), (hi[:, width:], lo[:, width:]))

    @pl.when(i == 0)
    def _():
        w_ref[...] = part

    @pl.when(i > 0)
    def _():
        w_ref[...] += part


def dense(cost_rows, a_blocks, a_cols, b_blocks, b_cols, orders):
    rows, width = cost_rows.shape
    nbx, nnza, blk, _ = a_blocks.shape
    nnzb = b_blocks.shape[1]
    step = 2 * blk
    total = width + orders
    return pl.pallas_call(
        functools.partial(dense_kernel, blk, step, nnza, nnzb, width),
        grid_spec=pltpu.PrefetchScalarGridSpec(
            num_scalar_prefetch=2,
            grid=(width // step,),
            in_specs=[
                pl.BlockSpec((2, nnza, blk, blk), lambda i, *_: (i, 0, 0, 0)),
                pl.BlockSpec((2, nnzb, blk, blk), lambda i, *_: (i, 0, 0, 0)),
                pl.BlockSpec((rows, step), lambda i, *_: (0, i)),
            ],
            out_specs=[
                pl.BlockSpec((step, total), lambda i, *_: (i, 0)),
                pl.BlockSpec((step, total), lambda i, *_: (i, 0)),
                pl.BlockSpec((rows, step), lambda i, *_: (0, i)),
                pl.BlockSpec((rows, step), lambda i, *_: (0, i)),
                pl.BlockSpec((rows, orders), lambda i, *_: (0, 0)),
            ],
            scratch_shapes=[pltpu.VMEM((step, total), F32)],
        ),
        out_shape=[
            jax.ShapeDtypeStruct((width, total), BF16),
            jax.ShapeDtypeStruct((width, total), BF16),
            jax.ShapeDtypeStruct((rows, width), BF16),
            jax.ShapeDtypeStruct((rows, width), BF16),
            jax.ShapeDtypeStruct((rows, orders), F32),
        ],
        compiler_params=pltpu.CompilerParams(vmem_limit_bytes=VMEM_LIMIT),
        cost_estimate=pl.CostEstimate(
            flops=6 * rows * width * orders, bytes_accessed=8 * width * total + 8 * rows * width, transcendentals=0
        ),
        name="dense",
    )(a_cols.reshape(-1), b_cols.reshape(-1), a_blocks, b_blocks, cost_rows)


def image_kernel(where, weight, fh, fl, ph, pl_, out, acc):
    k = pl.program_id(0)
    part = dot3((ph[...], pl_[...]), (fh[...], fl[...]))

    @pl.when(k == 0)
    def _():
        acc[...] = part

    @pl.when(k > 0)
    def _():
        acc[...] += part

    @pl.when(k == pl.num_programs(0) - 1)
    def _():
        out[...] = acc[...].T * weight[0]


def image(where, weight, fh, fl, ph, pl_):
    rows, width = ph.shape
    chunk = 512
    return pl.pallas_call(
        image_kernel,
        grid_spec=pltpu.PrefetchScalarGridSpec(
            num_scalar_prefetch=2,
            grid=(width // chunk,),
            in_specs=[
                pl.BlockSpec((chunk, rows), lambda k, where, _: (k, where[0])),
                pl.BlockSpec((chunk, rows), lambda k, where, _: (k, where[0])),
                pl.BlockSpec((rows, chunk), lambda k, *_: (0, k)),
                pl.BlockSpec((rows, chunk), lambda k, *_: (0, k)),
            ],
            out_specs=pl.BlockSpec((rows, rows), lambda k, *_: (0, 0)),
            scratch_shapes=[pltpu.VMEM((rows, rows), F32)],
        ),
        out_shape=jax.ShapeDtypeStruct((rows, rows), F32),
        compiler_params=pltpu.CompilerParams(vmem_limit_bytes=VMEM_LIMIT),
        cost_estimate=pl.CostEstimate(
            flops=6 * rows * rows * width, bytes_accessed=8 * rows * width, transcendentals=0
        ),
        name="image",
    )(where, weight, fh, fl, ph, pl_)


def gather_kernel(first, where, y_ref, fh, fl, *refs):
    out = refs[-1]
    part = dot3(split(y_ref[...]), (fh[...], fl[...]))
    out[...] = part if first else refs[0][...] + part


def accumulate(where, y, fh, fl, acc):
    rows = y.shape[0]
    total = fh.shape[1]
    tile = 512
    first = acc is None
    spec = pl.BlockSpec((rows, tile), lambda n, where: (0, n))
    factor = pl.BlockSpec((rows, tile), lambda n, where: (where[0], n))
    return pl.pallas_call(
        functools.partial(gather_kernel, first),
        grid_spec=pltpu.PrefetchScalarGridSpec(
            num_scalar_prefetch=1,
            grid=(total // tile,),
            in_specs=[pl.BlockSpec((rows, rows), lambda n, where: (0, 0)), factor, factor] + [spec] * (not first),
            out_specs=spec,
        ),
        out_shape=jax.ShapeDtypeStruct((rows, total), F32),
        input_output_aliases={} if first else {4: 0},
        compiler_params=pltpu.CompilerParams(vmem_limit_bytes=VMEM_LIMIT),
        cost_estimate=pl.CostEstimate(
            flops=6 * rows * rows * total, bytes_accessed=12 * rows * total, transcendentals=0
        ),
        name="accumulate",
    )(where, y, fh, fl, *(() if first else (acc,)))


def inverse_block(m):
    n = m.shape[0]
    sub = lax.broadcasted_iota(jnp.int32, (n, n), 0)
    lane = lax.broadcasted_iota(jnp.int32, (n, n), 1)
    for j in range(n):
        pivot = 1.0 / m[j : j + 1, j : j + 1]
        col = m[:, j : j + 1]
        row = jnp.where(lane[:1] == j, 1.0, m[j : j + 1, :]) * pivot
        m = jnp.where(sub == j, row, jnp.where(lane == j, 0.0, m) - col * row)
    return m


def inverse_kernel(blk, h_ref, out):
    n = h_ref.shape[0]
    dot = functools.partial(jnp.dot, precision=HIGHEST, preferred_element_type=F32)
    out[...] = h_ref[...]

    @pl.loop(0, n // blk)
    def _(b):
        here = pl.ds(pl.multiple_of(b * blk, blk), blk)
        inv = inverse_block(out[here, here])
        row = dot(inv, out[here, :])
        col = out[:, here]
        out[...] -= dot(col, row)
        out[:, here] = -dot(col, inv)
        out[here, :] = row
        out[here, here] = inv


def inverse(h, blk):
    n = h.shape[0]
    return pl.pallas_call(
        functools.partial(inverse_kernel, blk),
        out_shape=jax.ShapeDtypeStruct((n, n), F32),
        compiler_params=pltpu.CompilerParams(vmem_limit_bytes=VMEM_LIMIT),
        cost_estimate=pl.CostEstimate(flops=2**32, bytes_accessed=8 * n * n, transcendentals=n),
        name="inverse",
    )(h)


def final_kernel(where, s_ref, t_ref, k_ref, g_ref, d_ref, out):
    n = pl.program_id(0)
    rows = out.shape[0]
    part = s_ref[...] + t_ref[...] + dot3(split(k_ref[...]), split(g_ref[0]), NT)
    diag = lax.broadcasted_iota(jnp.int32, (rows, rows), 0) == lax.broadcasted_iota(jnp.int32, (rows, rows), 1)
    cost = jnp.where(diag & (n == where[0]), d_ref[...], 0.0)
    out[...] = part + cost


def final(where, own, other, gain_t, cross_t, state_cost):
    rows = own.shape[0]
    parts, _, orders = cross_t.shape
    spec = pl.BlockSpec((rows, rows), lambda n, where: (0, n))
    return pl.pallas_call(
        final_kernel,
        grid_spec=pltpu.PrefetchScalarGridSpec(
            num_scalar_prefetch=1,
            grid=(parts,),
            in_specs=[
                spec,
                spec,
                pl.BlockSpec((rows, orders), lambda n, where: (0, 0)),
                pl.BlockSpec((1, rows, orders), lambda n, where: (n, 0, 0)),
                pl.BlockSpec((1, rows), lambda n, where: (0, 0)),
            ],
            out_specs=spec,
        ),
        out_shape=jax.ShapeDtypeStruct((rows, parts * rows), F32),
        compiler_params=pltpu.CompilerParams(vmem_limit_bytes=VMEM_LIMIT),
        cost_estimate=pl.CostEstimate(
            flops=6 * rows * rows * parts * orders, bytes_accessed=16 * rows * rows * parts, transcendentals=0
        ),
        name="final",
    )(where, own, other, gain_t, cross_t, state_cost[None])


def swapped(x):
    n = lax.axis_size("leaf")
    return lax.ppermute(x, "leaf", [(i, i ^ 1) for i in range(n)])


def shards(
    leaf_cost,
    a_blocks,
    a_cols,
    b_blocks,
    b_cols,
    branch_prob,
    state_cost,
    control_cost,
    parent_state,
):
    rows, width = leaf_cost.shape[1:]
    blk = a_blocks.shape[3]
    orders = control_cost.shape[0]
    parts = lax.axis_size("row")
    z = lax.axis_index("row")
    leaf = lax.axis_index("leaf")
    core = leaf % 2
    weight = branch_prob[0]

    def halves(x, axis):
        size = x.shape[axis] // 2
        return lax.dynamic_slice_in_dim(x, core * size, size, axis)

    def joined(mine, axis):
        other = swapped(mine)
        first = jnp.where(core == 0, mine, other)
        second = jnp.where(core == 0, other, mine)
        return jnp.concatenate((first, second), axis)

    own_state = lax.dynamic_index_in_dim(parent_state, leaf // 2, 0, keepdims=False)
    full_state = joined(lax.all_gather(halves(own_state, 0), "row"), 1).reshape(width, -1)

    fh, fl, ph, pl_, w = dense(leaf_cost[0], a_blocks[0], a_cols[0], b_blocks[0], b_cols[0], orders)
    first = z * rows
    mine = lax.dynamic_slice_in_dim(fh, first, rows, 0), lax.dynamic_slice_in_dim(fl, first, rows, 0)
    a_mine = mine[0][:, :width], mine[1][:, :width]
    b_mine = mine[0][:, width:], mine[1][:, width:]

    arrived = []
    for d in list(range(1, parts)) + [0]:
        to = (z + d) % parts
        block = image(to[None], branch_prob, fh, fl, ph, pl_)
        if d:
            block = lax.ppermute(block, "row", [(i, (i + d) % parts) for i in range(parts)])
        arrived.append(((z - d) % parts, block))

    w_pair = parted(w)
    drift = dot3(a_mine, parted(full_state))
    gram = jnp.concatenate((dot3(b_mine, w_pair, TN), dot3(w_pair, parted(drift), TN)), axis=1) * weight
    gram = gram + swapped(gram)
    gram = joined(lax.psum(halves(gram, 0), "row"), 0)
    hinv = inverse(gram[:, :orders] + jnp.diag(control_cost), blk)
    order = -jnp.dot(hinv, gram[:, orders:], precision=HIGHEST)
    reached = drift + dot3(b_mine, parted(order))

    acc = None
    for source, block in arrived[-1:] + arrived[:-1]:
        acc = accumulate(source[None], block, fh, fl, acc)
    cross = acc[:, width:]
    cross = cross + swapped(cross)
    other = swapped(acc[:, :width])
    every = joined(lax.all_gather(halves(cross, 0), "row"), 1)
    gain_t = -jnp.dot(cross, hinv, precision=HIGHEST)
    pcost = final(z[None], acc, other, gain_t, every, state_cost)
    return pcost[None], gain_t.T[None], reached[None]


def solution(mesh):
    placed = (
        P("leaf", "row", None),
        P("leaf", None, None, None, None),
        P("leaf", None, None),
        P("leaf", None, None, None, None),
        P("leaf", None, None),
        P("leaf"),
        P("row"),
        P(),
        P(None, "row", None),
    )
    return jax.shard_map(
        shards,
        mesh=mesh,
        in_specs=placed,
        out_specs=(P("leaf", "row", None), P("leaf", None, "row"), P("leaf", "row", None)),
        check_vma=False,
    )
```

time: 763 us -> 356 us (0.47); the launches traced: 752 us -> 354 us
  waiting for transfers between devices: 287 us -> 119 us
  matrix products: 187 us -> 25.5 us
  Pallas kernels: 0 us -> 144 us
  other arithmetic: 134 us -> 10.8 us
  local copies, waits for them, and re-layouts: 127 us -> 17.3 us
  blocking collectives: 0 us -> 18 us
    pallas_call x0 -> x11, Pallas kernels: none -> 144 us  [the longest x1 50.1 us: inverse(): pl.pallas_call(functools.partial(inverse_kernel, blk), out_shape=jax.Shap...]
    dot_general x14, matrix products: 164 us -> 25.5 us  [the longest x12 21.5 us: dot3(): return one(a[0], b[0]) + (one(a[0], b[1]) + one(a[1], b[0]))]
    another operation x18 -> x0, other arithmetic: 123 us -> none  [the longest x14 80.4 us: shards(): factor = jnp.linalg.cholesky(gram_total)]
    reduce_scatter x1 -> x0, waiting for transfers between devices: 113 us -> none  [shards(): lax.psum_scatter(state_part, 'row', scatter_dimension=0, tiled=True)]
    psum x2 -> x1, waiting for transfers between devices: 147 us -> 43.1 us  [shards(): gram = joined(lax.psum(halves(gram, 0), 'row'), 0)]
    dot_general x2 -> x0, local copies, waits for them, and re-layouts: 44.9 us -> none  [the longest x1 34.5 us: shards(): a_pieces = jnp.einsum('rkb,ksbc->ksrc', cost_split, a_all, precision=HIGH)]
    another operation x37 -> x2, local copies, waits for them, and re-layouts: 30.4 us -> 0.17 us  [the longest x1 0.09 us: dense(): a_cols.reshape(-1)]
    ppermute x3 -> x9, waiting for transfers between devices: 0.01 us -> 28.4 us  [the longest x3 26.8 us: shards(): lax.ppermute(block, 'row', [(i, (i + d) % parts) for i in range(parts)])]
  transfers between devices with their start and end apart: 7 -> 11, of which waited for: 4 -> 5; matrix products, arithmetic and copies ran while one was open for 35% -> 13% of each run, Pallas kernels for 0% -> 38%
where the time goes in v1:
time: 356 us; the launch traced here: 354 us
  Pallas kernels  144 us (40%)
  waiting for transfers between devices  119 us (33%)
  matrix products  25.5 us (7%)
  blocking collectives  18 us (5%)
  local copies, waits for them, and re-layouts  17.3 us (5%)
  between operations  15 us (4%)
  other arithmetic  10.8 us (3%)
  starting transfers between devices  5.16 us (1%)
    pallas_call x1, Pallas kernels, inverse(): pl.pallas_call(functools.partial(inverse_kernel, blk), out_shape=jax.Shap...  50.1 us
    all_gather x1, waiting for transfers between devices, shards(): every = joined(lax.all_gather(halves(cross, 0), 'row'), 1)  47 us
    psum x1, waiting for transfers between devices, shards(): gram = joined(lax.psum(halves(gram, 0), 'row'), 0)  43.1 us
    pallas_call x4, Pallas kernels, accumulate(): pl.pallas_call(functools.partial(gather_kernel, first), grid_spec=pltpu.P...  38.3 us
    pallas_call x4, Pallas kernels, image(): pl.pallas_call(image_kernel, grid_spec=pltpu.PrefetchScalarGridSpec(num_s...  28 us
    ppermute x3, waiting for transfers between devices, shards(): lax.ppermute(block, 'row', [(i, (i + d) % parts) for i in range(parts)])  26.8 us
    dot_general x12, matrix products, dot3(): return one(a[0], b[0]) + (one(a[0], b[1]) + one(a[1], b[0]))  21.5 us
    pallas_call x1, Pallas kernels, dense(): pl.pallas_call(functools.partial(dense_kernel, blk, step, nnza, nnzb, wid...  18.7 us
  transfers between devices with their start and end apart: 11, of which 5 were waited for; matrix products, arithmetic and copies ran while one was open for 13% of the time, Pallas kernels for 38%

profile of v1, /device:TPU:0, one launch (start us, length us, event | category | flops | bytes accessed | tf_op | source)
XLA Modules:
  0.0 354.1 jit_solution(5474580170865527104)
XLA Ops:
  8.4 18.0 %all_gather.10 = f32[4,256,128]{2,1,0:T(8,128)} all-gather(f32[1,256,128]{2,1,0:T(8,128)S(1)} %constant_dynamic-slice_fusion.1), channel_id=1, replica_groups=mesh['leaf'=8,'row'=4] {'row'}, dimensions={0}, use_global_device_ids=true | all-gather | bytes 655360 | tf_op jit(solution)/shard_map/all_gather | solution.py:293
  28.8 18.7 %dense.1 = (bf16[2048,2560]{1,0:T(8,128)(2,1)}, bf16[2048,2560]{1,0:T(8,128)(2,1)}, bf16[512,2048]{1,0:T(8,128)(2,1)S(1)}, bf16[512,2048]{1,0:T(8,128)(2,1)S(1)}, f32[512,512]{1,0:T(8,128)S(1)}) custom-call(s32[128]{0:T(128)S(1)} %reshape_squeeze.6.acol, s32[32]{0:T(128)S(1)} %reshape_squeeze.7.bcol, f32[16,8,128,128]{3,2,1,0:T(8,128)} %bitcast.36, ...), custom_call_target="tpu_custom_call" | custom-call | flops 3221225472 | bytes 50331648 | tf_op jit(solution)/shard_map/dense/pallas_call | solution.py:73
  47.4 7.8 %image.4 = f32[512,512]{1,0:T(8,128)} custom-call(s32[1]{0:T(128)} %bitcast.2.where, f32[1]{0:T(128)} %copy.52.weight, bf16[2048,2560]{1,0:T(8,128)(2,1)} %get-tuple-element.8.fh, bf16[2048,2560]{1,0:T(8,128)(2,1)} %get-tuple-element.9.fl, bf16[512,2048]{1,0:T(8,128)(2,1)S(1)} %get-tuple-element.10.ph, bf16[512,2048]{1,0:T(8,128)(2,1)S(1)} %get-tuple-element.11.pl_), custom_call_target="tpu_custom_call" | custom-call | flops 3221225472 | bytes 8388608 | tf_op jit(solution)/shard_map/image/pallas_call | solution.py:127
  55.3 4.2 %collective-permute-start = (f32[512,512]{1,0:T(8,128)}, f32[512,512]{1,0:T(8,128)}, u32[]{:S(2)}, u32[]{:S(2)}) collective-permute-start(f32[512,512]{1,0:T(8,128)} %image.4), channel_id=1, source_target_pairs={{0,3},{1,0},{2,1},{3,2},{4,7},{5,4},{6,5},{7,6},{8,11},{9,8},{10,9... | collective-permute-start | bytes 3145736 | tf_op jit(solution)/shard_map/ppermute | solution.py:306
  61.1 7.1 %image.5 = f32[512,512]{1,0:T(8,128)} custom-call(s32[1]{0:T(128)} %bitcast.7.where, f32[1]{0:T(128)} %copy.52.weight, bf16[2048,2560]{1,0:T(8,128)(2,1)} %get-tuple-element.8.fh, bf16[2048,2560]{1,0:T(8,128)(2,1)} %get-tuple-element.9.fl, bf16[512,2048]{1,0:T(8,128)(2,1)S(1)} %get-tuple-element.10.ph, bf16[512,2048]{1,0:T(8,128)(2,1)S(1)} %copy-done.3), custom_call_target="tpu_custom_call" | custom-call | flops 3221225472 | bytes 8388608 | tf_op jit(solution)/shard_map/image/pallas_call | solution.py:127
  69.7 7.1 %image.6 = f32[512,512]{1,0:T(8,128)} custom-call(s32[1]{0:T(128)} %bitcast.9.where, f32[1]{0:T(128)} %copy.52.weight, bf16[2048,2560]{1,0:T(8,128)(2,1)} %get-tuple-element.8.fh, bf16[2048,2560]{1,0:T(8,128)(2,1)} %get-tuple-element.9.fl, bf16[512,2048]{1,0:T(8,128)(2,1)S(1)} %get-tuple-element.10.ph, bf16[512,2048]{1,0:T(8,128)(2,1)S(1)} %copy-done.4), custom_call_target="tpu_custom_call" | custom-call | flops 3221225472 | bytes 8388608 | tf_op jit(solution)/shard_map/image/pallas_call | solution.py:127
  78.2 2.5 fusion.24
  80.8 2.7 fusion.26
  83.4 3.5 fusion.6
  86.9 6.1 %image.7.y_ref = f32[512,512]{1,0:T(8,128)S(1)} custom-call(s32[1]{0:T(128)} %bitcast.10.where, f32[1]{0:T(128)} %copy.52.weight, bf16[2048,2560]{1,0:T(8,128)(2,1)} %get-tuple-element.8.fh, bf16[2048,2560]{1,0:T(8,128)(2,1)} %get-tuple-element.9.fl, bf16[512,2048]{1,0:T(8,128)(2,1)S(1)} %get-tuple-element.10.ph, bf16[512,2048]{1,0:T(8,128)(2,1)S(1)} %copy-done.5), custom_call_target="tpu_custom_call" | custom-call | flops 3221225472 | bytes 8388608 | tf_op jit(solution)/shard_map/image/pallas_call | solution.py:127
  95.2 8.4 %accumulate.4.refs_0_ = f32[512,2560]{1,0:T(8,128)} custom-call(s32[1]{0:T(128)} %bitcast.10.where, f32[512,512]{1,0:T(8,128)S(1)} %copy-done.7, bf16[2048,2560]{1,0:T(8,128)(2,1)} %get-tuple-element.8.fh, bf16[2048,2560]{1,0:T(8,128)(2,1)} %get-tuple-element.9.fl), custom_call_target="tpu_custom_call" | custom-call | flops 4026531840 | bytes 15728640 | tf_op jit(solution)/shard_map/accumulate/pallas_call | solution.py:163
  105.2 2.4 fusion
  109.9 2.4 fusion.7
  113.5 15.1 %collective-permute-done.2.y_ref = f32[512,512]{1,0:T(8,128)} collective-permute-done((f32[512,512]{1,0:T(8,128)}, f32[512,512]{1,0:T(8,128)}, u32[]{:S(2)}, u32[]{:S(2)}) %collective-permute-start.2) | collective-permute-done | bytes 1048608 | tf_op jit(solution)/shard_map/ppermute | solution.py:306
  128.6 10.0 %accumulate.5.refs_0_ = f32[512,2560]{1,0:T(8,128)} custom-call(s32[1]{0:T(128)} %bitcast.8.where, f32[512,512]{1,0:T(8,128)} %collective-permute-done.2.y_ref, bf16[2048,2560]{1,0:T(8,128)(2,1)} %get-tuple-element.8.fh, bf16[2048,2560]{1,0:T(8,128)(2,1)} %get-tuple-element.9.fl, f32[512,2560]{1,0:T(8,128)} %accumulate.4.refs_0_), custom_call_target="tpu_custom_call", output_to_operand_aliasing={{}: (4, {})} | custom-call | flops 4026531840 | bytes 15728640 | tf_op jit(solution)/shard_map/accumulate/pallas_call | solution.py:163
  138.6 11.6 %collective-permute-done.1.y_ref = f32[512,512]{1,0:T(8,128)} collective-permute-done((f32[512,512]{1,0:T(8,128)}, f32[512,512]{1,0:T(8,128)}, u32[]{:S(2)}, u32[]{:S(2)}) %collective-permute-start.1) | collective-permute-done | bytes 1048608 | tf_op jit(solution)/shard_map/ppermute | solution.py:306
  150.2 10.0 %accumulate.6.refs_0_ = f32[512,2560]{1,0:T(8,128)} custom-call(s32[1]{0:T(128)} %bitcast.6.where, f32[512,512]{1,0:T(8,128)} %collective-permute-done.1.y_ref, bf16[2048,2560]{1,0:T(8,128)(2,1)} %get-tuple-element.8.fh, bf16[2048,2560]{1,0:T(8,128)(2,1)} %get-tuple-element.9.fl, f32[512,2560]{1,0:T(8,128)} %accumulate.5.refs_0_), custom_call_target="tpu_custom_call", output_to_operand_aliasing={{}: (4, {})} | custom-call | flops 4026531840 | bytes 15728640 | tf_op jit(solution)/shard_map/accumulate/pallas_call | solution.py:163
  160.2 10.0 %accumulate.7.s_ref = f32[512,2560]{1,0:T(8,128)} custom-call(s32[1]{0:T(128)} %bitcast.1.where, f32[512,512]{1,0:T(8,128)} %collective-permute-done.y_ref, bf16[2048,2560]{1,0:T(8,128)(2,1)} %get-tuple-element.8.fh, bf16[2048,2560]{1,0:T(8,128)(2,1)} %get-tuple-element.9.fl, f32[512,2560]{1,0:T(8,128)} %accumulate.6.refs_0_), custom_call_target="tpu_custom_call", output_to_operand_aliasing={{}: (4, {})} | custom-call | flops 4026531840 | bytes 15728640 | tf_op jit(solution)/shard_map/accumulate/pallas_call | solution.py:163
  176.5 4.7 %slice.32 = f32[512,2048]{1,0:T(8,128)} slice(f32[512,2560]{1,0:T(8,128)} %accumulate.7.s_ref), slice={[0:512], [0:2048]} | slice | bytes 8388608 | tf_op jit(solution)/shard_map/slice | solution.py:323
  181.3 43.1 %all-reduce.2.cloned.1.call-done = f32[256,640]{1,0:T(8,128)} async-done(((f32[256,640]{1,0:T(8,128)}), f32[256,640]{1,0:T(8,128)}) %all-reduce.2.cloned.1.call-update) | async-done | bytes 655376 | tf_op jit(solution)/shard_map/psum | solution.py:313
  224.4 47.0 %all-gather.3.cloned.1.call-done = f32[1024,512]{1,0:T(8,128)} async-done(((f32[256,512]{1,0:T(8,128)}), f32[1024,512]{1,0:T(8,128)}) %all-gather.3.cloned.1.call-update) | async-done | bytes 2097168 | tf_op jit(solution)/shard_map/all_gather | solution.py:324
  273.7 50.1 %inverse.1 = f32[512,512]{1,0:T(8,128)S(1)} custom-call(f32[512,512]{1,0:T(8,128)S(1)} %fusion.16.h_ref), custom_call_target="tpu_custom_call" | custom-call | flops 4294967296 | bytes 2097152 | tf_op jit(solution)/shard_map/inverse/pallas_call | solution.py:212
  336.1 2.4 pad_maximum_fusion.g_ref
  338.5 8.7 %final.1 = f32[512,2048]{1,0:T(8,128)} custom-call(s32[1]{0:T(128)} %bitcast.where, f32[512,2560]{1,0:T(8,128)} %accumulate.7.s_ref, f32[512,2048]{1,0:T(8,128)} %collective-permute-done.3.t_ref, f32[512,512]{1,0:T(8,128)S(1)} %convolution_negate_fusion.k_ref, f32[4,512,512]{2,1,0:T(8,128)} %pad_maximum_fusion.g_ref, f32[1,512]{1,0:T(1,128)S(1)} %bitcast.35), custom_call_target="tpu_custom_call" | custom-call | flops 3221225472 | bytes 16777216 | tf_op jit(solution)/shard_map/final/pallas_call | solution.py:234
  (76 shorter events, 35.6 us)
Async XLA Ops:
  7.2 1.2 copy-start
  7.2 217.2 %all-reduce.2.cloned.1.call-start = ((), (), s32[]{:S(2)}) async-start(), calls=%async_computation | async-start | bytes 1310720 | tf_op jit(solution)/shard_map/psum | solution.py:313
  26.4 77.2 %collective-permute-start.5 = (f32[4,256,128]{2,1,0:T(8,128)}, f32[4,256,128]{2,1,0:T(8,128)}, u32[]{:S(2)}, u32[]{:S(2)}) collective-permute-start(f32[4,256,128]{2,1,0:T(8,128)} %all_gather.10), channel_id=1, source_target_pairs={{0,4},{4,0},{8,12},{12,8},{16,20},{20,16},{24,28},{28,24},{1,5},{5... | collective-permute-start | bytes 1572872 | tf_op jit(solution)/shard_map/ppermute | solution.py:259
  47.4 7.8 %copy-start.2 = (bf16[512,2048]{1,0:T(8,128)(2,1)}, bf16[512,2048]{1,0:T(8,128)(2,1)S(1)}, u32[]{:S(2)}) copy-start(bf16[512,2048]{1,0:T(8,128)(2,1)S(1)} %get-tuple-element.11.pl_) | copy-start | bytes 6291460
  55.3 104.9 %collective-permute-start = (f32[512,512]{1,0:T(8,128)}, f32[512,512]{1,0:T(8,128)}, u32[]{:S(2)}, u32[]{:S(2)}) collective-permute-start(f32[512,512]{1,0:T(8,128)} %image.4), channel_id=1, source_target_pairs={{0,3},{1,0},{2,1},{3,2},{4,7},{5,4},{6,5},{7,6},{8,11},{9,8},{10,9... | collective-permute-start | bytes 3145736 | tf_op jit(solution)/shard_map/ppermute | solution.py:306
  59.5 1.6 copy-start.3
  68.1 82.1 %collective-permute-start.1 = (f32[512,512]{1,0:T(8,128)}, f32[512,512]{1,0:T(8,128)}, u32[]{:S(2)}, u32[]{:S(2)}) collective-permute-start(f32[512,512]{1,0:T(8,128)} %image.5), channel_id=1, source_target_pairs={{0,2},{1,3},{2,0},{3,1},{4,6},{5,7},{6,4},{7,5},{8,10},{9,11},{10,... | collective-permute-start | bytes 3145736 | tf_op jit(solution)/shard_map/ppermute | solution.py:306
  68.1 1.6 copy-start.4
  76.8 51.8 %collective-permute-start.2 = (f32[512,512]{1,0:T(8,128)}, f32[512,512]{1,0:T(8,128)}, u32[]{:S(2)}, u32[]{:S(2)}) collective-permute-start(f32[512,512]{1,0:T(8,128)} %image.6), channel_id=1, source_target_pairs={{0,1},{1,2},{2,3},{3,0},{4,5},{5,6},{6,7},{7,4},{8,9},{9,10},{10,1... | collective-permute-start | bytes 3145736 | tf_op jit(solution)/shard_map/ppermute | solution.py:306
  83.4 3.5 copy-start.5
  94.0 1.2 copy-start.7
  105.2 7.1 %copy-start.9 = (bf16[512,512]{1,0:T(8,128)(2,1)S(1)}, bf16[512,512]{1,0:T(8,128)(2,1)}, u32[]{:S(2)}) copy-start(bf16[512,512]{1,0:T(8,128)(2,1)} %reduce-precision_convert_fusion.1) | copy-start | bytes 1572868
  109.9 3.4 copy-start.12
  113.4 58.1 %collective-permute-start.6 = (f32[512,640]{1,0:T(8,128)S(1)}, f32[512,640]{1,0:T(8,128)S(1)}, u32[]{:S(2)}, u32[]{:S(2)}) collective-permute-start(f32[512,640]{1,0:T(8,128)S(1)} %maximum_multiply_fusion), channel_id=1, source_target_pairs={{0,4},{4,0},{8,12},{12,8},{16,20},{20,16},{24,28},{28,24},{1,5},{5... | collective-permute-start | bytes 3932168 | tf_op jit(solution)/shard_map/ppermute | solution.py:259
  171.4 2.7 collective-permute-start.4
  172.5 99.0 %all-gather.3.cloned.1.call-start = ((), (), s32[]{:S(2)}) async-start(), calls=%async_computation.1 | async-start | bytes 2621440 | tf_op jit(solution)/shard_map/all_gather | solution.py:324
  176.5 97.0 %copy-start.14 = (f32[512]{0:T(512)S(1)}, f32[512]{0:T(512)}, u32[]{:S(2)}) copy-start(f32[512]{0:T(512)} %param.16) | copy-start | bytes 6148
  181.2 157.4 %collective-permute-start.3 = (f32[512,2048]{1,0:T(8,128)}, f32[512,2048]{1,0:T(8,128)}, u32[]{:S(2)}, u32[]{:S(2)}) collective-permute-start(f32[512,2048]{1,0:T(8,128)} %slice.32), channel_id=1, source_target_pairs={{0,4},{4,0},{8,12},{12,8},{16,20},{20,16},{24,28},{28,24},{1,5},{5... | collective-permute-start | bytes 12582920 | tf_op jit(solution)/shard_map/ppermute | solution.py:259
  224.4 47.1 %collective-permute-start.7 = (f32[256,640]{1,0:T(8,128)}, f32[256,640]{1,0:T(8,128)S(1)}, u32[]{:S(2)}, u32[]{:S(2)}) collective-permute-start(f32[256,640]{1,0:T(8,128)} %all-reduce.2.cloned.1.call-done), channel_id=1, source_target_pairs={{0,4},{4,0},{8,12},{12,8},{16,20},{20,16},{24,28},{28,24},{1,5},{5... | collective-permute-start | bytes 1966088 | tf_op jit(solution)/shard_map/ppermute | solution.py:259
  271.4 62.4 %collective-permute-start.8 = (f32[4,256,512]{2,1,0:T(8,128)}, f32[4,256,512]{2,1,0:T(8,128)}, u32[]{:S(2)}, u32[]{:S(2)}) collective-permute-start(f32[4,256,512]{2,1,0:T(8,128)} %bitcast.39), channel_id=1, source_target_pairs={{0,4},{4,0},{8,12},{12,8},{16,20},{20,16},{24,28},{28,24},{1,5},{5... | collective-permute-start | bytes 6291464 | tf_op jit(solution)/shard_map/ppermute | solution.py:259
  272.6 51.2 %copy-start.11 = (f32[256,640]{1,0:T(8,128)}, f32[256,640]{1,0:T(8,128)S(1)}, u32[]{:S(2)}) copy-start(f32[256,640]{1,0:T(8,128)S(1)} %get-tuple-element.25) | copy-start | bytes 1966084
  327.0 6.9 %copy-start.13 = (f32[1024,512]{1,0:T(8,128)S(1)}, f32[1024,512]{1,0:T(8,128)}, u32[]{:S(2)}) copy-start(f32[1024,512]{1,0:T(8,128)} %all-gather.3.cloned.1.call-done) | copy-start | bytes 6291460
  336.1 2.4 copy-start.8
  338.5 8.7 %copy-start.1 = (f32[4,512,128]{2,1,0:T(8,128)S(1)}, f32[4,512,128]{2,1,0:T(8,128)}, u32[]{:S(2)}) copy-start(f32[4,512,128]{2,1,0:T(8,128)} %param.17) | copy-start | bytes 3145732
  (2 other events, 1.9 us)
Sparse Core Ops, SparseCore 0:
  172.6 51.7 all-reduce.1
  226.0 45.4 all-gather.2
